TPU v7x, 512 devices: a whole 4x4x16 slice. The times are simulated.
512 devices in a mesh: mem: 8 (over z_lo), space: 64 (over z_hi, x, y, core).
Axes of the slice: x: 4, y: 4, z: 16 (z_hi: 2, z_lo: 8; z = z_hi * 8 + z_lo), core: 2. Of those that a mesh axis runs over, the one named last changes fastest.
Arguments:
- gradient: bfloat16 [6, 2, 768, 1536], P(None, None, 'space', 'mem'), may hold values from -6 to 6
- perturbations: bfloat16 [16, 6, 2, 768, 1536], P('mem', None, None, 'space'), may hold values from -6 to 6
- band_index: int32 [768, 1536], P('space'), may hold values from 0 to 15
- band_weight: float32 [16], replicated, may hold values from 0.3 to 3
- wave_index: int32 [768, 768], P('space'), may hold values from 0 to 767
- spectrum: float32 [2, 768], replicated, may hold values from 0.3 to 3
Outputs:
- control_grad: float32 [16, 2, 1536, 768], P('mem', None, 'space')
All inputs are finite; a program needn't handle non-finite values.
Results may differ from a plain program's by a relative error of at most 0.0058.
Values may be sent and summed in bfloat16 or wider, within the bound.
A program may use at most 64 MiB of HBM per device.

v0:
```python
import math

import jax
import jax.numpy as jnp
from jax import lax
from jax.sharding import PartitionSpec as P

NLAT = 768
MT = 768
NDEG = 768


def zonal_table(nlon, waves):
    lon_index = jnp.arange(nlon, dtype=jnp.int32)[:, None]
    column = jnp.arange(2 * waves, dtype=jnp.int32)[None, :]
    wavenumber = column // 2
    phase = lon_index * wavenumber % nlon
    angle = phase.astype(jnp.float32) * jnp.float32(2.0 * math.pi / nlon)
    values = jnp.where(column % 2 == 0, jnp.cos(angle), -jnp.sin(angle))
    return (values * jnp.float32(math.sqrt(2.0 / nlon))).astype(jnp.bfloat16)


def latitude_basis(nlat, degrees):
    cycle = jnp.arange(nlat, dtype=jnp.int32)[:, None]
    degree = jnp.arange(degrees, dtype=jnp.int32)[None, :]
    phase = degree * (2 * cycle + 1) % (4 * nlat)
    angle = phase.astype(jnp.float32) * jnp.float32(math.pi / (2 * nlat))
    return (jnp.cos(angle) * jnp.float32(math.sqrt(2.0 / nlat))).astype(jnp.bfloat16)


def body(gradient, perturbations, band_index, band_weight, wave_index, spectrum):
    members, fields, levels, cycles, nlon = perturbations.shape
    spaces = lax.axis_size("space")
    bands = band_weight.shape[0]
    band_ids = jnp.arange(bands, dtype=jnp.int32)
    area = jnp.sum(
        jnp.where(band_index[:, :, None] == band_ids, band_weight, jnp.float32(0.0)), axis=-1
    )
    table = zonal_table(nlon, MT)
    gathered = lax.all_gather(gradient, "mem", axis=3, tiled=True)
    mixed = jnp.sum(perturbations.astype(jnp.float32) * gathered.astype(jnp.float32)[None], axis=1)
    alpha_grad = (area * mixed).astype(jnp.bfloat16)
    zonal_float = jnp.einsum("elji,iq->eljq", alpha_grad, table, preferred_element_type=jnp.float32)
    zonal_terms = zonal_float.astype(jnp.bfloat16)
    basis = latitude_basis(NLAT, NDEG)
    basis_view = basis.reshape(spaces, cycles, NDEG)
    local_modes = 2 * MT // spaces
    factor = jnp.repeat(jnp.take(spectrum, wave_index, axis=1), 2, axis=1)
    outputs = []
    for level_index in range(levels):

        def latitude_level(received, level_index=level_index):
            count = received.shape[0]
            shaped = received.reshape(count, cycles, spaces, local_modes)
            summed = jnp.einsum(
                "ejsq,sjk->eqk", shaped, basis_view, preferred_element_type=jnp.float32
            )
            return summed * factor[level_index][None]

        outputs.append(
            latitude_level(
                lax.all_to_all(
                    zonal_terms[:, level_index], "space", split_axis=2, concat_axis=2, tiled=True
                )
            )
        )
    return jnp.stack(outputs, axis=1)


def solution(mesh):
    in_specs = (
        P(None, None, "space", "mem"),
        P("mem", None, None, "space", None),
        P("space", None),
        P(),
        P("space", None),
        P(),
    )
    out_specs = P("mem", None, "space", None)
    return jax.shard_map(body, mesh=mesh, in_specs=in_specs, out_specs=out_specs, check_vma=False)
```

profile of v0, /device:TPU:1, one launch (start us, length us, event | category | flops | bytes accessed | tf_op | source)
XLA Modules:
  0.0 270.4 jit_solution(13298965982332019888)
XLA Ops:
  0.0 1.3 copy.42
  1.4 100.4 %all_gather.3 = bf16[6,2,12,1536]{2,1,0,3:T(2,128)(2,1)} all-gather(bf16[6,2,12,192]{2,1,0,3:T(2,128)(2,1)S(1)} %copy.42), channel_id=1, replica_groups=mesh['mem'=8,'space'=64] {'mem'}, dimensions={3}, use_global_device_ids=true | all-gather | bytes 497664 | tf_op jit(solution)/shard_map/all_gather | solution.py:40
  101.7 11.0 %copy.43 = bf16[6,2,12,1536]{3,1,2,0:T(2,128)(2,1)S(1)} copy(bf16[6,2,12,1536]{2,1,0,3:T(2,128)(2,1)} %all_gather.3) | data formatting | bytes 884736 | tf_op jit(solution)/shard_map/all_gather | solution.py:40
  112.8 0.0 copy-start.2
  112.8 0.0 copy-start.4
  112.8 0.3 convert_element_type.31
  113.1 1.0 multiply_reduce_fusion
  114.2 0.3 select_reduce_fusion
  114.5 0.1 multiply_convert_fusion.1
  114.6 40.5 %fusion.17 = bf16[2,2,12,1536]{3,2,1,0:T(8,128)(2,1)S(1)} fusion(s32[1536]{0:T(1024)S(1)} %add_select_fusion.2, pred[1536]{0:T(1024)(128)(4,1)S(1)} %fusion.50, bf16[2,2,12,1536]{3,1,2,0:T(2,128)(2,1)S(1)} %multiply_convert_fusion.1), kind=kOutput, calls=%fused_computation.22 | convolution fusion | flops 257236992 | bytes 302592 | tf_op jit(solution)/shard_map/elji,iq->eljq/dot_general | solution.py:43
  155.2 0.0 copy-start.1
  155.2 0.0 copy-start.3
  155.2 0.6 copy.50
  155.9 1.6 reshape.109
  157.5 19.3 %all-to-all-start.1 = ((bf16[64,2,288]{2,1,0:T(2,128)(2,1)}), bf16[64,2,288]{2,1,0:T(2,128)(2,1)S(1)}, u32[]{:S(2)}, u32[]{:S(2)}) async-start(bf16[64,2,288]{2,1,0:T(2,128)(2,1)} %reshape.109), calls=%async_computation.1 | async-start | bytes 196608 | tf_op jit(solution)/shard_map/all_to_all | solution.py:62
  176.9 0.2 copy.48
  177.1 31.0 %gather_fusion = f32[9216,2]{1,0:T(8,128)} fusion(f32[2,768]{0,1:T(8,128)S(1)} %copy.48, s32[9216]{0:T(1024)S(1)} %broadcast_clamp_fusion), kind=kCustom, calls=%fused_computation | custom fusion | bytes 184320 | tf_op jit(solution)/shard_map/jit(_take)/gather | solution.py:48
  208.1 3.5 %copy.49 = f32[12,768,2]{1,0,2:T(8,128)S(1)} copy(f32[12,768,2]{2,1,0:T(8,128)} %bitcast.62) | data formatting | bytes 147456 | tf_op jit(solution)/shard_map/jit(_take)/gather | solution.py:48
  211.6 0.6 copy.45
  212.2 1.6 reshape.111
  213.8 0.0 all-to-all-done.1
  213.8 17.6 %all-to-all-start = ((bf16[64,2,288]{2,1,0:T(2,128)(2,1)}), bf16[64,2,288]{2,1,0:T(2,128)(2,1)S(1)}, u32[]{:S(2)}, u32[]{:S(2)}) async-start(bf16[64,2,288]{2,1,0:T(2,128)(2,1)} %reshape.111), calls=%async_computation | async-start | bytes 196608 | tf_op jit(solution)/shard_map/all_to_all | solution.py:62
  231.5 0.1 broadcast_in_dim.54
  231.6 0.1 broadcast_in_dim.52
  231.7 0.7 reshape.110
  232.4 1.8 copy.57
  234.2 14.2 %all-to-all-done = bf16[64,2,288]{2,1,0:T(2,128)(2,1)S(1)} async-done(((bf16[64,2,288]{2,1,0:T(2,128)(2,1)}), bf16[64,2,288]{2,1,0:T(2,128)(2,1)S(1)}, u32[]{:S(2)}, u32[]{:S(2)}) %all-to-all-start) | async-done | bytes 73760 | tf_op jit(solution)/shard_map/all_to_all | solution.py:62
  248.4 0.7 reshape.112
  249.1 1.8 copy.55
  250.9 9.2 %fusion.40 = f32[2,1,24,768]{3,2,0,1:T(8,128)S(1)} fusion(bf16[2,12,64,24]{3,2,0,1:T(8,128)(2,1)S(1)} %copy.57, s32[64,12]{0,1:T(8,128)S(1)} %multiply_add_fusion, f32[24,768]{1,0:T(8,128)S(1)} %broadcast_in_dim.54), kind=kOutput, calls=%fused_computation.38 | convolution fusion | flops 63148032 | bytes 297984 | tf_op jit(solution)/shard_map/ejsq,sjk->eqk/dot_general | solution.py:55
  260.1 9.3 %fusion.46 = f32[2,1,24,768]{3,2,0,1:T(8,128)S(1)} fusion(bf16[2,12,64,24]{3,2,0,1:T(8,128)(2,1)S(1)} %copy.55, s32[64,12]{0,1:T(8,128)S(1)} %multiply_add_fusion, f32[24,768]{1,0:T(8,128)S(1)} %broadcast_in_dim.52), kind=kOutput, calls=%fused_computation.40 | convolution fusion | flops 63148032 | bytes 297984 | tf_op jit(solution)/shard_map/ejsq,sjk->eqk/dot_general | solution.py:55
  269.5 0.7 copy.53
  (19 shorter events, 0.2 us)
Async XLA Ops:
  101.7 11.4 %copy-start = (bf16[2,6,2,12,1536]{4,2,3,1,0:T(2,128)(2,1)S(1)}, bf16[2,6,2,12,1536]{4,2,3,1,0:T(2,128)(2,1)}, u32[]{:S(2)}) copy-start(bf16[2,6,2,12,1536]{4,2,3,1,0:T(2,128)(2,1)} %param.7) | copy-start | bytes 2654212
  112.8 1.4 copy-start.2
  112.8 1.4 copy-start.4
  155.2 21.6 %copy-start.1 = (s32[12,768]{1,0:T(8,128)S(1)}, s32[12,768]{1,0:T(8,128)}, u32[]{:S(2)}) copy-start(s32[12,768]{1,0:T(8,128)} %param.10) | copy-start | bytes 110596
  155.2 21.7 %copy-start.3 = (f32[2,768]{1,0:T(2,128)S(1)}, f32[2,768]{1,0:T(2,128)}, u32[]{:S(2)}) copy-start(f32[2,768]{1,0:T(2,128)} %param.11) | copy-start | bytes 18436
  157.5 56.4 %all-to-all-start.1 = ((bf16[64,2,288]{2,1,0:T(2,128)(2,1)}), bf16[64,2,288]{2,1,0:T(2,128)(2,1)S(1)}, u32[]{:S(2)}, u32[]{:S(2)}) async-start(bf16[64,2,288]{2,1,0:T(2,128)(2,1)} %reshape.109), calls=%async_computation.1 | async-start | bytes 196608 | tf_op jit(solution)/shard_map/all_to_all | solution.py:62
  213.8 34.6 %all-to-all-start = ((bf16[64,2,288]{2,1,0:T(2,128)(2,1)}), bf16[64,2,288]{2,1,0:T(2,128)(2,1)S(1)}, u32[]{:S(2)}, u32[]{:S(2)}) async-start(bf16[64,2,288]{2,1,0:T(2,128)(2,1)} %reshape.111), calls=%async_computation | async-start | bytes 196608 | tf_op jit(solution)/shard_map/all_to_all | solution.py:62
where the time goes:
time: 273 us; the launch traced here: 270 us
  blocking collectives  100 us (37%)
  matrix products  59 us (22%)
  local copies, waits for them, and re-layouts  57.4 us (21%)
  starting transfers between devices  37 us (14%)
  waiting for transfers between devices  14.2 us (5%)
    all_gather x1, blocking collectives, body(): gathered = lax.all_gather(gradient, 'mem', axis=3, tiled=True)  100 us
    dot_general x1, matrix products, body(): jnp.einsum('elji,iq->eljq', alpha_grad, table, preferred_element_type=jnp...  40.5 us
    all_to_all x2, starting transfers between devices, body(): lax.all_to_all(zonal_terms[:, level_index], 'space', split_axis=2, concat...  37 us
    gather x2, local copies, waits for them, and re-layouts, body(): factor = jnp.repeat(jnp.take(spectrum, wave_index, axis=1), 2, axis=1)  34.5 us
    dot_general x2, matrix products, latitude_level(): jnp.einsum('ejsq,sjk->eqk', shaped, basis_view, preferred_element_type=jn...  18.5 us
    all_to_all x2, waiting for transfers between devices, body(): lax.all_to_all(zonal_terms[:, level_index], 'space', split_axis=2, concat...  14.2 us
    all_gather x1, local copies, waits for them, and re-layouts, body(): gathered = lax.all_gather(gradient, 'mem', axis=3, tiled=True)  11 us
    unnamed x16, local copies, waits for them, and re-layouts  6.06 us
  transfers between devices with their start and end apart: 2, of which 1 were waited for; matrix products, arithmetic and copies ran while one was open for 15% of the time, Pallas kernels for 0%

commit v1 on v0

v1 whole, which is shorter than its diff:
```python
import functools
import math

import jax
import jax.numpy as jnp
import ml_dtypes
import numpy as np
from jax import lax
from jax.experimental import pallas as pl
from jax.experimental.pallas import tpu as pltpu
from jax.sharding import PartitionSpec as P

MESH = pl.DeviceIdType.MESH
BF16 = jnp.bfloat16
F32 = jnp.float32

MEMS = 8
HALF = 32
NLAT = 768
NLON = 1536
MT = 768
NDEG = 768
CYC = 12
FIELDS = 6
ROWS = 144
GROWS = 224

def gather_trees():
    trees = []
    for s in range(MEMS):
        tree = {n: [] for n in range(MEMS)}
        near = range(0, 4) if s < 4 else range(4, 8)
        relay = s + 4 if s < 4 else s - 4
        far = range(4, 8) if s < 4 else range(0, 4)
        tree[s] = [relay] + sorted((n for n in near if n != s), key=lambda n: -abs(n - s))
        tree[relay] = sorted((n for n in far if n != relay), key=lambda n: -abs(n - relay))
        trees.append(tree)
    return trees


def zonal_constant():
    phase = (np.arange(NLON)[:, None] * np.arange(MT)[None, :]) % NLON
    angle = phase * (2.0 * math.pi / NLON)
    pair = np.stack([np.cos(angle), -np.sin(angle)], axis=-1).reshape(NLON, 2 * MT)
    pair = (pair * math.sqrt(2.0 / NLON)).astype(np.float32).astype(ml_dtypes.bfloat16)
    return np.ascontiguousarray(pair.reshape(NLON, 2, MT).transpose(1, 0, 2))


def latitude_constant():
    phase = (np.arange(NDEG)[None, :] * (2 * np.arange(NLAT)[:, None] + 1)) % (4 * NLAT)
    basis = np.cos(phase * (math.pi / (2 * NLAT))) * math.sqrt(2.0 / NLAT)
    padded = np.zeros((2, HALF, 16, NDEG), np.float32)
    padded[:, :, :CYC] = basis.reshape(2, HALF, CYC, NDEG)
    return padded.reshape(2, HALF * 16, NDEG).astype(ml_dtypes.bfloat16)


def spread_constant():
    place = np.zeros((HALF * 24, HALF * 32), np.float32)
    for d in range(HALF):
        place[d * 24 + np.arange(24), d * 32 + np.arange(24)] = 1.0
    return place.astype(ml_dtypes.bfloat16)


def kernel(
    trees,
    weight_s, grad_h, pert_h, band_h, wave_h, spec_h, table_h, basis_h, place_h,
    out_ref,
    grad_v, pert_v, band_v, wave_v, spec_v, table_v, basis_v, place_v,
    gpack, ppack, area, factor, gbuf, alpha, zsend, zrecv, send, recv,
    load_sem, gs_sem, gr_sem, as_sem, ar_sem, bs_sem, br_sem,
):
    m = lax.axis_index("mem")
    space = lax.axis_index("space")
    zh = space // HALF
    s32 = space % HALF
    partner = (1 - zh) * HALF + s32

    loads = [
        (grad_h, grad_v), (pert_h, pert_v), (band_h, band_v), (wave_h, wave_v), (spec_h, spec_v),
        (table_h.at[1 - zh], table_v.at[0]), (table_h.at[zh], table_v.at[1]), (place_h, place_v),
        (basis_h, basis_v),
    ]
    loads = [pltpu.make_async_copy(a, b, load_sem.at[i]) for i, (a, b) in enumerate(loads)]
    for c in loads:
        c.start()

    barrier = pltpu.get_barrier_semaphore()

    def greet(d, _):
        pl.semaphore_signal(barrier, inc=1, device_id=((m + d) % MEMS, space), device_id_type=MESH)
        return 0

    lax.fori_loop(1, MEMS, greet, 0)
    pl.semaphore_signal(barrier, inc=1, device_id=(m, partner), device_id_type=MESH)

    def greet_half(d, _):
        pl.semaphore_signal(
            barrier, inc=1, device_id=(m, zh * HALF + (s32 + d) % HALF), device_id_type=MESH
        )
        return 0

    lax.fori_loop(1, HALF, greet_half, 0)

    loads[0].wait()
    for f in range(FIELDS):
        for l in range(2):
            v = grad_v[f, l].astype(F32)
            gpack[f * 24 + 8 * l : f * 24 + 8 * l + 8, 0:192] = v[0:8]
            gpack[f * 24 + 16 + 4 * l : f * 24 + 20 + 4 * l, 0:192] = v[8:12]
    lane = lax.broadcasted_iota(jnp.int32, (ROWS, 128), 1)
    low = lane < 64
    t0 = gpack[:, 0:128]
    t1 = gpack[:, 128:256]
    odd = m % 2
    full = jnp.where(odd == 1, jnp.where(low, pltpu.roll(t0, 64, 1), pltpu.roll(t1, 64, 1)), t0)
    part = jnp.where(odd == 1, t0, t1)
    turned = pltpu.roll(part, 64, 1)
    low72 = low[0:72]
    folded = jnp.where(
        odd == 1,
        jnp.where(low72, part[72:144], turned[0:72]),
        jnp.where(low72, part[0:72], turned[72:144]),
    )
    gbuf[m, 0:144] = full.astype(BF16)
    gbuf[m, 144:224] = jnp.concatenate([folded, jnp.zeros((8, 128), F32)], axis=0).astype(BF16)

    pl.semaphore_wait(barrier, MEMS - 1 + 1 + HALF - 1)

    def gather_copy(s, child, index):
        return pltpu.make_async_remote_copy(
            gbuf.at[s], gbuf.at[s], gs_sem.at[index], gr_sem.at[s],
            device_id=(child, space), device_id_type=MESH,
        )

    first = [[(k, c) for c in trees[k][k]] for k in range(MEMS)]
    later = []
    for k in range(MEMS):
        order = sorted((s for s in range(MEMS) if s != k), key=lambda s: (s not in near_of(trees, k), abs(s - k)))
        later.append(order)

    for k in range(MEMS):
        @pl.when(m == k)
        def _(k=k):
            for i, (s, c) in enumerate(first[k]):
                gather_copy(s, c, i).start()

    loads[2].wait()
    band = band_v[...]
    a = jnp.zeros((CYC, NLON), F32)
    for b in range(16):
        a = jnp.where(band == b, weight_s[b], a)
    area[0:8] = a[0:8]
    area[8:16] = a[0:8]
    area[16:20] = a[8:12]
    area[20:24] = a[8:12]

    loads[1].wait()
    for e in range(2):
        for f in range(FIELDS):
            for l in range(2):
                v = pert_v[e, f, l].astype(F32)
                ppack[e, f * 24 + 8 * l : f * 24 + 8 * l + 8] = v[0:8]
                ppack[e, f * 24 + 16 + 4 * l : f * 24 + 20 + 4 * l] = v[8:12]

    loads[3].wait()
    loads[4].wait()
    for t in range(6):
        idx = wave_v[:, t * 128 : t * 128 + 128]
        block = idx // 128
        place = idx % 128
        for l in range(2):
            got = jnp.zeros((CYC, 128), F32)
            for b in range(6):
                row = jnp.broadcast_to(spec_v[l : l + 1, b * 128 : b * 128 + 128], (CYC, 128))
                got = jnp.where(block == b, jnp.take_along_axis(row, place, axis=1), got)
            for r in range(CYC):
                factor[l, 2 * r : 2 * r + 2, t * 128 : t * 128 + 128] = jnp.broadcast_to(
                    got[r : r + 1], (2, 128)
                )

    for k in range(MEMS):
        @pl.when(m == k)
        def _(k=k):
            sent = list(first[k])
            for s in later[k]:
                gather_copy(s, 0, 0).wait_recv()
                for c in trees[s][k]:
                    gather_copy(s, c, len(sent)).start()
                    sent.append((s, c))
            for i, (s, c) in enumerate(sent):
                gather_copy(s, c, i).wait_send()

    low = low72
    for p in range(4):
        ge = gbuf[2 * p].astype(F32)
        go = gbuf[2 * p + 1].astype(F32)
        fe, fo = ge[144:216], go[144:216]
        mid = jnp.concatenate(
            [jnp.where(low, fe, fo), pltpu.roll(jnp.where(low, fo, fe), 64, 1)], axis=0
        )
        for t, tile in enumerate((ge[0:144], mid, go[0:144])):
            lanes = slice((3 * p + t) * 128, (3 * p + t) * 128 + 128)
            rows = []
            for e in range(2):
                acc = ppack[e, 0:24, lanes] * tile[0:24]
                for f in range(1, FIELDS):
                    acc = acc + ppack[e, f * 24 : f * 24 + 24, lanes] * tile[f * 24 : f * 24 + 24]
                rows.append(area[:, lanes] * acc)
            alpha[:, lanes] = jnp.concatenate(rows, axis=0).astype(BF16)

    loads[5].wait()
    zsend[...] = jnp.dot(alpha[...], table_v[0], preferred_element_type=F32).astype(BF16)
    across = pltpu.make_async_remote_copy(
        zsend, zrecv, as_sem, ar_sem, device_id=(m, partner), device_id_type=MESH
    )
    across.start()
    loads[6].wait()
    mine = jnp.dot(alpha[...], table_v[1], preferred_element_type=F32).astype(BF16)

    lane = lax.broadcasted_iota(jnp.int32, (16, 128), 1)
    sub = lax.broadcasted_iota(jnp.int32, (8, 128), 0)

    def message(zs, peer):
        return pltpu.make_async_remote_copy(
            send.at[zs, peer], recv.at[zs, s32], bs_sem.at[zs], br_sem.at[zs],
            device_id=(m, zh * HALF + peer), device_id_type=MESH,
        )

    def spread(z, zs):
        y = jnp.dot(z, place_v[...], preferred_element_type=F32)
        for t in range(8):
            yt = y[:, t * 128 : t * 128 + 128]
            blocks = []
            for e in range(2):
                for l in range(2):
                    top = yt[(3 * e + l) * 8 : (3 * e + l) * 8 + 8]
                    rest = yt[(3 * e + 2) * 8 : (3 * e + 2) * 8 + 8]
                    if l == 1:
                        rest = pltpu.roll(rest, 4, 0)
                    rest = jnp.where(sub < 4, rest, 0.0)
                    blocks.append(jnp.concatenate([top, rest], axis=0))
            for d in range(4):
                whole = None
                for el in range(4):
                    shift = (32 * (el - d)) % 128
                    moved = pltpu.roll(blocks[el], shift, 1) if shift else blocks[el]
                    whole = moved if whole is None else jnp.where(lane >= 32 * el, moved, whole)
                send[zs, 4 * t + d] = whole.astype(BF16)
        recv[zs, s32] = send[zs, s32]

        def go(d, _):
            message(zs, (s32 + d) % HALF).start()
            return 0

        lax.fori_loop(1, HALF, go, 0)

    def arrived(zs):
        pltpu.make_async_copy(send.at[zs, 0:31], recv.at[zs, 0:31], br_sem.at[zs]).wait()

    def left(zs):
        pltpu.make_async_copy(send.at[zs, 0:31], recv.at[zs, 0:31], bs_sem.at[zs]).wait()

    loads[7].wait()
    spread(mine, zh)
    across.wait_recv()
    spread(zrecv[...], 1 - zh)

    loads[8].wait()
    arrived(zh)
    dims = (((0,), (0,)), ((), ()))
    total = lax.dot_general(
        recv[zh].reshape(HALF * 16, 128), basis_v[zh], dims, preferred_element_type=F32
    )
    arrived(1 - zh)
    total = total + lax.dot_general(
        recv[1 - zh].reshape(HALF * 16, 128), basis_v[1 - zh], dims, preferred_element_type=F32
    )
    for e in range(2):
        for l in range(2):
            el = 2 * e + l
            out_ref[e, l] = total[el * 32 : el * 32 + 24] * factor[l]

    across.wait_send()
    left(zh)
    left(1 - zh)


def near_of(trees, k):
    return [s for s in range(MEMS) if k in trees[s][s]]


def body(gradient, perturbations, band_index, band_weight, wave_index, spectrum):
    trees = gather_trees()
    table = jnp.asarray(zonal_constant())
    basis = jnp.asarray(latitude_constant())
    place = jnp.asarray(spread_constant())
    hbm = pl.BlockSpec(memory_space=pl.ANY)
    dma = pltpu.SemaphoreType.DMA
    return pl.pallas_call(
        functools.partial(kernel, trees),
        name="alpha_adjoint",
        out_shape=jax.ShapeDtypeStruct((2, 2, 24, NDEG), F32),
        in_specs=[pl.BlockSpec(memory_space=pltpu.SMEM)] + [hbm] * 8,
        out_specs=pl.BlockSpec(memory_space=pltpu.VMEM),
        scratch_shapes=[
            pltpu.VMEM(gradient.shape, BF16),
            pltpu.VMEM(perturbations.shape, BF16),
            pltpu.VMEM(band_index.shape, jnp.int32),
            pltpu.VMEM(wave_index.shape, jnp.int32),
            pltpu.VMEM(spectrum.shape, F32),
            pltpu.VMEM(table.shape, BF16),
            pltpu.VMEM(basis.shape, BF16),
            pltpu.VMEM(place.shape, BF16),
            pltpu.VMEM((ROWS, 256), F32),
            pltpu.VMEM((2, ROWS, NLON), F32),
            pltpu.VMEM((24, NLON), F32),
            pltpu.VMEM((2, 24, NDEG), F32),
            pltpu.VMEM((MEMS, GROWS, 128), BF16),
            pltpu.VMEM((48, NLON), BF16),
            pltpu.VMEM((48, MT), BF16),
            pltpu.VMEM((48, MT), BF16),
            pltpu.VMEM((2, HALF, 16, 128), BF16),
            pltpu.VMEM((2, HALF, 16, 128), BF16),
            dma((9,)),
            dma((24,)),
            dma((MEMS,)),
            dma,
            dma,
            dma((2,)),
            dma((2,)),
        ],
        compiler_params=pltpu.CompilerParams(
            collective_id=0, has_side_effects=True, vmem_limit_bytes=40 * 2**20
        ),
    )(band_weight, gradient, perturbations, band_index, wave_index, spectrum, table, basis, place)


def solution(mesh):
    in_specs = (
        P(None, None, "space", "mem"),
        P("mem", None, None, "space", None),
        P("space", None),
        P(),
        P("space", None),
        P(),
    )
    out_specs = P("mem", None, "space", None)
    return jax.shard_map(body, mesh=mesh, in_specs=in_specs, out_specs=out_specs, check_vma=False)
```

time: 273 us -> 56.7 us (0.21)
  blocking collectives: 100 us -> 0 us
  matrix products: 59 us -> 0 us
  local copies, waits for them, and re-layouts: 57.4 us -> 6.83 us
  Pallas kernels: 0 us -> 49.6 us
  starting transfers between devices: 37 us -> 0 us
  waiting for transfers between devices: 14.2 us -> 0 us
    all_gather x1 -> x0, blocking collectives: 100 us -> none  [body(): gathered = lax.all_gather(gradient, 'mem', axis=3, tiled=True)]
    dot_general x3 -> x0, matrix products: 59 us -> none  [the longest x1 40.5 us: body(): jnp.einsum('elji,iq->eljq', alpha_grad, table, preferred_element_type=jnp...]
    pallas_call x0 -> x1, Pallas kernels: none -> 49.6 us  [body(): pl.pallas_call(functools.partial(kernel, trees), name='alpha_adjoint', ou...]
    all_to_all x2 -> x0, starting transfers between devices: 37 us -> none  [body(): lax.all_to_all(zonal_terms[:, level_index], 'space', split_axis=2, concat...]
    gather x2 -> x0, local copies, waits for them, and re-layouts: 34.5 us -> none  [body(): factor = jnp.repeat(jnp.take(spectrum, wave_index, axis=1), 2, axis=1)]
    all_to_all x2 -> x0, waiting for transfers between devices: 14.2 us -> none  [body(): lax.all_to_all(zonal_terms[:, level_index], 'space', split_axis=2, concat...]
    all_gather x1 -> x0, local copies, waits for them, and re-layouts: 11 us -> none  [body(): gathered = lax.all_gather(gradient, 'mem', axis=3, tiled=True)]
    reshape x2 -> x0, local copies, waits for them, and re-layouts: 3.6 us -> none  [latitude_level(): shaped = received.reshape(count, cycles, spaces, local_modes)]
  transfers between devices with their start and end apart: 2 -> 0, of which waited for: 1 -> 0; matrix products, arithmetic and copies ran while one was open for 15% -> 0% of each run, Pallas kernels for 0% -> 0%
where the time goes in v1:
time: 56.7 us; the launch traced here: 56.5 us
  Pallas kernels  49.6 us (87%)
  local copies, waits for them, and re-layouts  6.83 us (12%)
    pallas_call x1, Pallas kernels, body(): pl.pallas_call(functools.partial(kernel, trees), name='alpha_adjoint', ou...  49.6 us
    unnamed x17, local copies, waits for them, and re-layouts  6.83 us

profile of v1, /device:TPU:1, one launch (start us, length us, event | category | flops | bytes accessed | tf_op | source)
XLA Modules:
  0.0 56.5 jit_solution(13225952137525866499)
XLA Ops:
  0.0 0.0 copy-start.1
  0.0 0.0 copy-start.5
  0.0 0.0 copy-start.4
  0.0 0.0 copy-start.6
  0.0 0.0 copy-start.3
  0.0 1.0 %copy.10.grad_h = bf16[6,2,12,192]{3,2,1,0:T(8,128)(2,1)S(1)} copy(bf16[6,2,12,192]{3,1,2,0:T(2,128)(2,1)} %param.9) | data formatting | bytes 110592 | tf_op args[0]
  1.1 1.3 %copy.11.pert_h = bf16[2,6,2,12,1536]{4,3,2,1,0:T(8,128)(2,1)S(1)} copy(bf16[2,6,2,12,1536]{4,2,3,1,0:T(2,128)(2,1)} %param.10) | data formatting | bytes 1769472 | tf_op args[1]
  2.4 0.0 copy-done.1
  2.4 0.0 copy-done.5
  2.4 0.0 copy-done.4
  2.4 0.0 copy-done.6
  2.4 0.0 copy-done.3
  2.4 0.0 copy-start
  2.5 2.3 %copy-done = bf16[2,1536,768]{2,1,0:T(8,128)(2,1)S(1)} copy-done((bf16[2,1536,768]{2,1,0:T(8,128)(2,1)S(1)}, bf16[2,1536,768]{2,1,0:T(8,128)(2,1)}, u32[]{:S(2)}) %copy-start) | copy-done | bytes 4718616
  4.8 0.0 copy-start.2
  4.8 1.4 %copy-done.2 = bf16[2,512,768]{2,1,0:T(8,128)(2,1)S(1)} copy-done((bf16[2,512,768]{2,1,0:T(8,128)(2,1)S(1)}, bf16[2,512,768]{2,1,0:T(8,128)(2,1)}, u32[]{:S(2)}) %copy-start.2) | copy-done | bytes 1572888
  6.2 49.6 %alpha_adjoint.1 = f32[2,2,24,768]{3,2,1,0:T(8,128)S(1)} custom-call(f32[16]{0:T(128)S(1)} %copy-done.6, bf16[6,2,12,192]{3,2,1,0:T(8,128)(2,1)S(1)} %copy.10.grad_h, bf16[2,6,2,12,1536]{4,3,2,1,0:T(8,128)(2,1)S(1)} %copy.11.pert_h, s32[12,1536]{1,0:T(8,128)S(1)} %copy-done.3, s32[12,768]{1,0:T(8,128)S(1)} %copy-done.4, f32[2,768]{1,0:T(2,128)S(1)} %copy-done.5, ...), custom_call_target="tpu_custom_call" | custom-call | tf_op jit(solution)/shard_map/alpha_adjoint/pallas_call | solution.py:299
  55.8 0.7 %copy.13 = f32[2,2,24,768]{3,2,1,0:T(8,128)} copy(f32[2,2,24,768]{3,2,1,0:T(8,128)S(1)} %alpha_adjoint.1) | data formatting | bytes 589824
Async XLA Ops:
  0.0 2.4 %copy-start.1 = (bf16[768,1024]{1,0:T(8,128)(2,1)S(1)}, bf16[768,1024]{1,0:T(8,128)(2,1)}, u32[]{:S(2)}) copy-start(bf16[768,1024]{1,0:T(8,128)(2,1)} %constant.8.clone.place_h) | copy-start | bytes 4718596
  0.0 2.4 %copy-start.5 = (f32[2,768]{1,0:T(2,128)S(1)}, f32[2,768]{1,0:T(2,128)}, u32[]{:S(2)}) copy-start(f32[2,768]{1,0:T(2,128)} %spec_h.1) | copy-start | bytes 18436
  0.0 2.4 %copy-start.4 = (s32[12,768]{1,0:T(8,128)S(1)}, s32[12,768]{1,0:T(8,128)}, u32[]{:S(2)}) copy-start(s32[12,768]{1,0:T(8,128)} %wave_h.1) | copy-start | bytes 110596
  0.0 2.4 %copy-start.6 = (f32[16]{0:T(128)S(1)}, f32[16]{0:T(128)}, u32[]{:S(2)}) copy-start(f32[16]{0:T(128)} %weight_s.1) | copy-start | bytes 196
  0.0 2.4 %copy-start.3 = (s32[12,1536]{1,0:T(8,128)S(1)}, s32[12,1536]{1,0:T(8,128)}, u32[]{:S(2)}) copy-start(s32[12,1536]{1,0:T(8,128)} %band_h.1) | copy-start | bytes 221188
  2.4 2.3 %copy-start = (bf16[2,1536,768]{2,1,0:T(8,128)(2,1)S(1)}, bf16[2,1536,768]{2,1,0:T(8,128)(2,1)}, u32[]{:S(2)}) copy-start(bf16[2,1536,768]{2,1,0:T(8,128)(2,1)} %constant.6.clone.table_h) | copy-start | bytes 14155780
  4.8 1.4 %copy-start.2 = (bf16[2,512,768]{2,1,0:T(8,128)(2,1)S(1)}, bf16[2,512,768]{2,1,0:T(8,128)(2,1)}, u32[]{:S(2)}) copy-start(bf16[2,512,768]{2,1,0:T(8,128)(2,1)} %constant.7.clone.basis_h) | copy-start | bytes 4718596

commit v2 on v1

--- a/solution.py
+++ b/solution.py
@@ -61,12 +61,21 @@
     return place.astype(ml_dtypes.bfloat16)
 
 
+def order_constant():
+    order = np.zeros((64, 48), np.float32)
+    for e in range(2):
+        for l in range(2):
+            for j in range(CYC):
+                order[(2 * e + l) * 16 + j, e * 24 + 2 * j + l] = 1.0
+    return order.astype(ml_dtypes.bfloat16)
+
+
 def kernel(
     trees,
-    weight_s, grad_h, pert_h, band_h, wave_h, spec_h, table_h, basis_h, place_h,
+    weight_s, grad_h, pert_h, band_h, wave_h, spec_h, table_h, basis_h, place_h, order_v,
     out_ref,
     grad_v, pert_v, band_v, wave_v, spec_v, table_v, basis_v, place_v,
-    gpack, ppack, area, factor, gbuf, alpha, zsend, zrecv, send, recv,
+    gpack, area, factor, gbuf, alpha, zsend, zrecv, send, recv,
     load_sem, gs_sem, gr_sem, as_sem, ar_sem, bs_sem, br_sem,
 ):
     m = lax.axis_index("mem")
@@ -76,7 +85,7 @@
     partner = (1 - zh) * HALF + s32
 
     loads = [
-        (grad_h, grad_v), (pert_h, pert_v), (band_h, band_v), (wave_h, wave_v), (spec_h, spec_v),
+        (grad_h.reshape(ROWS, 192), grad_v), (pert_h.reshape(2, ROWS, NLON), pert_v), (band_h, band_v), (wave_h, wave_v), (spec_h, spec_v),
         (table_h.at[1 - zh], table_v.at[0]), (table_h.at[zh], table_v.at[1]), (place_h, place_v),
         (basis_h, basis_v),
     ]
@@ -102,11 +111,7 @@
     lax.fori_loop(1, HALF, greet_half, 0)
 
     loads[0].wait()
-    for f in range(FIELDS):
-        for l in range(2):
-            v = grad_v[f, l].astype(F32)
-            gpack[f * 24 + 8 * l : f * 24 + 8 * l + 8, 0:192] = v[0:8]
-            gpack[f * 24 + 16 + 4 * l : f * 24 + 20 + 4 * l, 0:192] = v[8:12]
+    gpack[:, 0:192] = grad_v[...].astype(F32)
     lane = lax.broadcasted_iota(jnp.int32, (ROWS, 128), 1)
     low = lane < 64
     t0 = gpack[:, 0:128]
@@ -149,18 +154,8 @@
     a = jnp.zeros((CYC, NLON), F32)
     for b in range(16):
         a = jnp.where(band == b, weight_s[b], a)
-    area[0:8] = a[0:8]
-    area[8:16] = a[0:8]
-    area[16:20] = a[8:12]
-    area[20:24] = a[8:12]
-
-    loads[1].wait()
-    for e in range(2):
-        for f in range(FIELDS):
-            for l in range(2):
-                v = pert_v[e, f, l].astype(F32)
-                ppack[e, f * 24 + 8 * l : f * 24 + 8 * l + 8] = v[0:8]
-                ppack[e, f * 24 + 16 + 4 * l : f * 24 + 20 + 4 * l] = v[8:12]
+    for j in range(CYC):
+        area[2 * j : 2 * j + 2] = jnp.broadcast_to(a[j : j + 1], (2, NLON))
 
     loads[3].wait()
     loads[4].wait()
@@ -190,6 +185,7 @@
             for i, (s, c) in enumerate(sent):
                 gather_copy(s, c, i).wait_send()
 
+    loads[1].wait()
     low = low72
     for p in range(4):
         ge = gbuf[2 * p].astype(F32)
@@ -202,9 +198,10 @@
             lanes = slice((3 * p + t) * 128, (3 * p + t) * 128 + 128)
             rows = []
             for e in range(2):
-                acc = ppack[e, 0:24, lanes] * tile[0:24]
+                pert = pert_v[e, :, lanes].astype(F32)
+                acc = pert[0:24] * tile[0:24]
                 for f in range(1, FIELDS):
-                    acc = acc + ppack[e, f * 24 : f * 24 + 24, lanes] * tile[f * 24 : f * 24 + 24]
+                    acc = acc + pert[f * 24 : f * 24 + 24] * tile[f * 24 : f * 24 + 24]
                 rows.append(area[:, lanes] * acc)
             alpha[:, lanes] = jnp.concatenate(rows, axis=0).astype(BF16)
 
@@ -218,7 +215,6 @@
     mine = jnp.dot(alpha[...], table_v[1], preferred_element_type=F32).astype(BF16)
 
     lane = lax.broadcasted_iota(jnp.int32, (16, 128), 1)
-    sub = lax.broadcasted_iota(jnp.int32, (8, 128), 0)
 
     def message(zs, peer):
         return pltpu.make_async_remote_copy(
@@ -227,18 +223,10 @@
         )
 
     def spread(z, zs):
+        z = jnp.dot(order_v[...], z, preferred_element_type=F32).astype(BF16)
         y = jnp.dot(z, place_v[...], preferred_element_type=F32)
         for t in range(8):
-            yt = y[:, t * 128 : t * 128 + 128]
-            blocks = []
-            for e in range(2):
-                for l in range(2):
-                    top = yt[(3 * e + l) * 8 : (3 * e + l) * 8 + 8]
-                    rest = yt[(3 * e + 2) * 8 : (3 * e + 2) * 8 + 8]
-                    if l == 1:
-                        rest = pltpu.roll(rest, 4, 0)
-                    rest = jnp.where(sub < 4, rest, 0.0)
-                    blocks.append(jnp.concatenate([top, rest], axis=0))
+            blocks = [y[16 * el : 16 * el + 16, t * 128 : t * 128 + 128] for el in range(4)]
             for d in range(4):
                 whole = None
                 for el in range(4):
@@ -294,17 +282,20 @@
     table = jnp.asarray(zonal_constant())
     basis = jnp.asarray(latitude_constant())
     place = jnp.asarray(spread_constant())
+    order = jnp.asarray(order_constant())
+    gradient = gradient.transpose(0, 2, 1, 3)
+    perturbations = perturbations.transpose(0, 1, 3, 2, 4)
     hbm = pl.BlockSpec(memory_space=pl.ANY)
     dma = pltpu.SemaphoreType.DMA
     return pl.pallas_call(
         functools.partial(kernel, trees),
         name="alpha_adjoint",
         out_shape=jax.ShapeDtypeStruct((2, 2, 24, NDEG), F32),
-        in_specs=[pl.BlockSpec(memory_space=pltpu.SMEM)] + [hbm] * 8,
+        in_specs=[pl.BlockSpec(memory_space=pltpu.SMEM)] + [hbm] * 8 + [pl.BlockSpec(memory_space=pltpu.VMEM)],
         out_specs=pl.BlockSpec(memory_space=pltpu.VMEM),
         scratch_shapes=[
-            pltpu.VMEM(gradient.shape, BF16),
-            pltpu.VMEM(perturbations.shape, BF16),
+            pltpu.VMEM((ROWS, 192), BF16),
+            pltpu.VMEM((2, ROWS, NLON), BF16),
             pltpu.VMEM(band_index.shape, jnp.int32),
             pltpu.VMEM(wave_index.shape, jnp.int32),
             pltpu.VMEM(spectrum.shape, F32),
@@ -312,7 +303,6 @@
             pltpu.VMEM(basis.shape, BF16),
             pltpu.VMEM(place.shape, BF16),
             pltpu.VMEM((ROWS, 256), F32),
-            pltpu.VMEM((2, ROWS, NLON), F32),
             pltpu.VMEM((24, NLON), F32),
             pltpu.VMEM((2, 24, NDEG), F32),
             pltpu.VMEM((MEMS, GROWS, 128), BF16),
@@ -330,9 +320,9 @@
             dma((2,)),
         ],
         compiler_params=pltpu.CompilerParams(
-            collective_id=0, has_side_effects=True, vmem_limit_bytes=40 * 2**20
+            collective_id=0, has_side_effects=True, vmem_limit_bytes=60 * 2**20
         ),
-    )(band_weight, gradient, perturbations, band_index, wave_index, spectrum, table, basis, place)
+    )(band_weight, gradient, perturbations, band_index, wave_index, spectrum, table, basis, place, order)
 
 
 def solution(mesh):

time: 56.7 us -> 51.4 us (0.907)
  local copies, waits for them, and re-layouts: 6.83 us -> 1.69 us
    unnamed x17 -> x1, local copies, waits for them, and re-layouts: 6.83 us -> 1.69 us
where the time goes in v2:
time: 51.4 us; the launch traced here: 51.2 us
  Pallas kernels  49.5 us (96%)
  local copies, waits for them, and re-layouts  1.69 us (3%)
    pallas_call x1, Pallas kernels, body(): pl.pallas_call(functools.partial(kernel, trees), name='alpha_adjoint', ou...  49.5 us
    unnamed x1, local copies, waits for them, and re-layouts  1.69 us

profile of v2, /device:TPU:1, one launch (start us, length us, event | category | flops | bytes accessed | tf_op | source)
XLA Modules:
  0.0 51.2 jit_solution(10254959262110023358)
XLA Ops:
  0.0 49.5 %alpha_adjoint.1 = f32[2,2,24,768]{3,2,1,0:T(8,128)} custom-call(f32[16]{0:T(128)} %weight_s.1, bf16[6,12,2,192]{3,2,1,0:T(2,128)(2,1)} %bitcast.3, bf16[2,6,12,2,1536]{4,3,2,1,0:T(2,128)(2,1)} %bitcast.2, s32[12,1536]{1,0:T(8,128)} %band_h.1, s32[12,768]{1,0:T(8,128)} %wave_h.1, f32[2,768]{1,0:T(2,128)} %spec_h.1, ...), custom_call_target="tpu_custom_call" | custom-call | tf_op jit(solution)/shard_map/alpha_adjoint/pallas_call | solution.py:290
  49.5 1.7 %copy.12 = f32[2,2,24,768]{3,2,1,0:T(8,128)} copy(f32[2,2,24,768]{3,2,1,0:T(8,128)} %alpha_adjoint.1) | data formatting | bytes 589824

commit v3 on v2

--- a/solution.py
+++ b/solution.py
@@ -24,18 +24,39 @@
 FIELDS = 6
 ROWS = 144
 GROWS = 224
+REACH = 4
+RING = 16
+
+PARENTS = (
+    (0, 0, 1, 4, 0, 3, 4, 4),
+    (1, 1, 1, 1, 5, 2, 5, 5),
+    (2, 0, 2, 2, 6, 6, 2, 6),
+    (2, 0, 3, 3, 3, 7, 7, 3),
+)
+
 
 def gather_trees():
-    trees = []
+    parents = [list(p) for p in PARENTS]
+    for s in reversed(range(4)):
+        parents.append([7 - PARENTS[s][7 - n] for n in range(MEMS)])
+    children = [
+        [[c for c in range(MEMS) if c != s and parents[s][c] == n] for n in range(MEMS)] for s in range(MEMS)
+    ]
+    depths = []
     for s in range(MEMS):
-        tree = {n: [] for n in range(MEMS)}
-        near = range(0, 4) if s < 4 else range(4, 8)
-        relay = s + 4 if s < 4 else s - 4
-        far = range(4, 8) if s < 4 else range(0, 4)
-        tree[s] = [relay] + sorted((n for n in near if n != s), key=lambda n: -abs(n - s))
-        tree[relay] = sorted((n for n in far if n != relay), key=lambda n: -abs(n - relay))
-        trees.append(tree)
-    return trees
+        row = []
+        for n in range(MEMS):
+            depth = 0
+            while n != s:
+                assert abs(n - parents[s][n]) <= REACH
+                n = parents[s][n]
+                depth += 1
+            row.append(depth)
+        depths.append(row)
+    for s in range(MEMS):
+        for n in range(MEMS):
+            children[s][n].sort(key=lambda c: (-len(children[s][c]), -abs(c - n)))
+    return children, depths
 
 
 def zonal_constant():
@@ -55,8 +76,8 @@
 
 
 def spread_constant():
-    place = np.zeros((HALF * 24, HALF * 32), np.float32)
-    for d in range(HALF):
+    place = np.zeros((16 * 24, 16 * 32), np.float32)
+    for d in range(16):
         place[d * 24 + np.arange(24), d * 32 + np.arange(24)] = 1.0
     return place.astype(ml_dtypes.bfloat16)
 
@@ -76,31 +97,31 @@
     out_ref,
     grad_v, pert_v, band_v, wave_v, spec_v, table_v, basis_v, place_v,
     gpack, area, factor, gbuf, alpha, zsend, zrecv, send, recv,
-    load_sem, gs_sem, gr_sem, as_sem, ar_sem, bs_sem, br_sem,
+    load_sem, gs_sem, gr_sem, as_sem, ar_sem, bs_sem, br_sem, ready,
 ):
     m = lax.axis_index("mem")
     space = lax.axis_index("space")
     zh = space // HALF
     s32 = space % HALF
-    partner = (1 - zh) * HALF + s32
+    z = zh * MEMS + m
+
+    def along(d, place=None):
+        to = (z + d + RING) % RING
+        return to % MEMS, to // MEMS * HALF + (s32 if place is None else place)
 
     loads = [
-        (grad_h.reshape(ROWS, 192), grad_v), (pert_h.reshape(2, ROWS, NLON), pert_v), (band_h, band_v), (wave_h, wave_v), (spec_h, spec_v),
-        (table_h.at[1 - zh], table_v.at[0]), (table_h.at[zh], table_v.at[1]), (place_h, place_v),
-        (basis_h, basis_v),
+        (grad_h.reshape(ROWS, 192), grad_v), (band_h, band_v), (wave_h, wave_v), (spec_h, spec_v),
+        (pert_h.reshape(2, ROWS, NLON), pert_v), (table_h.at[1 - zh], table_v.at[0]),
+        (table_h.at[zh], table_v.at[1]), (place_h, place_v), (basis_h.at[zh], basis_v.at[0]),
+        (basis_h.at[1 - zh], basis_v.at[1]),
     ]
     loads = [pltpu.make_async_copy(a, b, load_sem.at[i]) for i, (a, b) in enumerate(loads)]
     for c in loads:
         c.start()
 
     barrier = pltpu.get_barrier_semaphore()
-
-    def greet(d, _):
-        pl.semaphore_signal(barrier, inc=1, device_id=((m + d) % MEMS, space), device_id_type=MESH)
-        return 0
-
-    lax.fori_loop(1, MEMS, greet, 0)
-    pl.semaphore_signal(barrier, inc=1, device_id=(m, partner), device_id_type=MESH)
+    for d in (4, -4, 3, -3, 2, -2, 1, -1):
+        pl.semaphore_signal(barrier, inc=1, device_id=along(d), device_id_type=MESH)
 
     def greet_half(d, _):
         pl.semaphore_signal(
@@ -129,7 +150,7 @@
     gbuf[m, 0:144] = full.astype(BF16)
     gbuf[m, 144:224] = jnp.concatenate([folded, jnp.zeros((8, 128), F32)], axis=0).astype(BF16)
 
-    pl.semaphore_wait(barrier, MEMS - 1 + 1 + HALF - 1)
+    pl.semaphore_wait(barrier, 2 * REACH + HALF - 1)
 
     def gather_copy(s, child, index):
         return pltpu.make_async_remote_copy(
@@ -137,19 +158,17 @@
             device_id=(child, space), device_id_type=MESH,
         )
 
-    first = [[(k, c) for c in trees[k][k]] for k in range(MEMS)]
-    later = []
-    for k in range(MEMS):
-        order = sorted((s for s in range(MEMS) if s != k), key=lambda s: (s not in near_of(trees, k), abs(s - k)))
-        later.append(order)
-
+    children, depths = trees
     for k in range(MEMS):
         @pl.when(m == k)
         def _(k=k):
-            for i, (s, c) in enumerate(first[k]):
-                gather_copy(s, c, i).start()
-
-    loads[2].wait()
+            for i, c in enumerate(children[k][k]):
+                gather_copy(k, c, i).start()
+
+    for d in (4, -4, 1, -1):
+        pl.semaphore_signal(ready, inc=1, device_id=along(d), device_id_type=MESH)
+
+    loads[1].wait()
     band = band_v[...]
     a = jnp.zeros((CYC, NLON), F32)
     for b in range(16):
@@ -157,8 +176,8 @@
     for j in range(CYC):
         area[2 * j : 2 * j + 2] = jnp.broadcast_to(a[j : j + 1], (2, NLON))
 
+    loads[2].wait()
     loads[3].wait()
-    loads[4].wait()
     for t in range(6):
         idx = wave_v[:, t * 128 : t * 128 + 128]
         block = idx // 128
@@ -173,19 +192,25 @@
                     got[r : r + 1], (2, 128)
                 )
 
+    def passes(k):
+        order = [s for s in range(MEMS) if s != k and children[s][k]]
+        order.sort(key=lambda s: (depths[s][k], abs(s - k)))
+        return order, [s for s in range(MEMS) if s != k and not children[s][k]]
+
     for k in range(MEMS):
         @pl.when(m == k)
         def _(k=k):
-            sent = list(first[k])
-            for s in later[k]:
+            count = len(children[k][k])
+            through, last = passes(k)
+            for s in through:
                 gather_copy(s, 0, 0).wait_recv()
-                for c in trees[s][k]:
-                    gather_copy(s, c, len(sent)).start()
-                    sent.append((s, c))
-            for i, (s, c) in enumerate(sent):
-                gather_copy(s, c, i).wait_send()
-
-    loads[1].wait()
+                for c in children[s][k]:
+                    gather_copy(s, c, count).start()
+                    count += 1
+            for s in last:
+                gather_copy(s, 0, 0).wait_recv()
+
+    loads[4].wait()
     low = low72
     for p in range(4):
         ge = gbuf[2 * p].astype(F32)
@@ -205,27 +230,34 @@
                 rows.append(area[:, lanes] * acc)
             alpha[:, lanes] = jnp.concatenate(rows, axis=0).astype(BF16)
 
+    pl.semaphore_wait(ready, 4)
     loads[5].wait()
-    zsend[...] = jnp.dot(alpha[...], table_v[0], preferred_element_type=F32).astype(BF16)
-    across = pltpu.make_async_remote_copy(
-        zsend, zrecv, as_sem, ar_sem, device_id=(m, partner), device_id_type=MESH
-    )
-    across.start()
+    across = []
+    for i, d in enumerate((7, -7)):
+        part = jnp.dot(alpha[...], table_v[0, :, i * 384 : i * 384 + 384], preferred_element_type=F32)
+        zsend[i] = part.astype(BF16)
+        across.append(
+            pltpu.make_async_remote_copy(
+                zsend.at[i], zrecv.at[i], as_sem.at[i], ar_sem.at[i],
+                device_id=along(d), device_id_type=MESH,
+            )
+        )
+        across[i].start()
     loads[6].wait()
     mine = jnp.dot(alpha[...], table_v[1], preferred_element_type=F32).astype(BF16)
 
     lane = lax.broadcasted_iota(jnp.int32, (16, 128), 1)
 
-    def message(zs, peer):
+    def message(kind, slot, to):
         return pltpu.make_async_remote_copy(
-            send.at[zs, peer], recv.at[zs, s32], bs_sem.at[zs], br_sem.at[zs],
-            device_id=(m, zh * HALF + peer), device_id_type=MESH,
-        )
-
-    def spread(z, zs):
-        z = jnp.dot(order_v[...], z, preferred_element_type=F32).astype(BF16)
-        y = jnp.dot(z, place_v[...], preferred_element_type=F32)
-        for t in range(8):
+            send.at[kind, slot], recv.at[kind, s32], bs_sem.at[kind], br_sem.at[kind],
+            device_id=to, device_id_type=MESH,
+        )
+
+    def spread(part, kind, base):
+        part = jnp.dot(order_v[...], part, preferred_element_type=F32).astype(BF16)
+        y = jnp.dot(part, place_v[...], preferred_element_type=F32)
+        for t in range(4):
             blocks = [y[16 * el : 16 * el + 16, t * 128 : t * 128 + 128] for el in range(4)]
             for d in range(4):
                 whole = None
@@ -233,48 +265,57 @@
                     shift = (32 * (el - d)) % 128
                     moved = pltpu.roll(blocks[el], shift, 1) if shift else blocks[el]
                     whole = moved if whole is None else jnp.where(lane >= 32 * el, moved, whole)
-                send[zs, 4 * t + d] = whole.astype(BF16)
-        recv[zs, s32] = send[zs, s32]
-
-        def go(d, _):
-            message(zs, (s32 + d) % HALF).start()
-            return 0
-
-        lax.fori_loop(1, HALF, go, 0)
-
-    def arrived(zs):
-        pltpu.make_async_copy(send.at[zs, 0:31], recv.at[zs, 0:31], br_sem.at[zs]).wait()
-
-    def left(zs):
-        pltpu.make_async_copy(send.at[zs, 0:31], recv.at[zs, 0:31], bs_sem.at[zs]).wait()
+                slot = base + 4 * t + d
+                send[kind, slot] = whole.astype(BF16)
+                if kind == 0:
+                    @pl.when(s32 != slot)
+                    def _(slot=slot):
+                        message(0, slot, (m, zh * HALF + slot)).start()
+                else:
+                    message(1, slot, along(1 if base == 0 else -1, slot)).start()
+
+    def arrived(kind, count):
+        pltpu.make_async_copy(send.at[kind, 0:count], recv.at[kind, 0:count], br_sem.at[kind]).wait()
+
+    def left(kind, count):
+        pltpu.make_async_copy(send.at[kind, 0:count], recv.at[kind, 0:count], bs_sem.at[kind]).wait()
 
     loads[7].wait()
-    spread(mine, zh)
-    across.wait_recv()
-    spread(zrecv[...], 1 - zh)
+    spread(mine[:, 0:384], 0, 0)
+    spread(mine[:, 384:768], 0, 16)
+    recv[0, s32] = send[0, s32]
+    for i in range(2):
+        across[i].wait_recv()
+        spread(zrecv[i], 1, 16 * i)
 
     loads[8].wait()
-    arrived(zh)
+    arrived(0, HALF - 1)
     dims = (((0,), (0,)), ((), ()))
     total = lax.dot_general(
-        recv[zh].reshape(HALF * 16, 128), basis_v[zh], dims, preferred_element_type=F32
+        recv[0].reshape(HALF * 16, 128), basis_v[0], dims, preferred_element_type=F32
     )
-    arrived(1 - zh)
+    loads[9].wait()
+    arrived(1, HALF)
     total = total + lax.dot_general(
-        recv[1 - zh].reshape(HALF * 16, 128), basis_v[1 - zh], dims, preferred_element_type=F32
+        recv[1].reshape(HALF * 16, 128), basis_v[1], dims, preferred_element_type=F32
     )
     for e in range(2):
         for l in range(2):
             el = 2 * e + l
             out_ref[e, l] = total[el * 32 : el * 32 + 24] * factor[l]
 
-    across.wait_send()
-    left(zh)
-    left(1 - zh)
-
-
-def near_of(trees, k):
-    return [s for s in range(MEMS) if k in trees[s][s]]
+    for k in range(MEMS):
+        @pl.when(m == k)
+        def _(k=k):
+            count = 0
+            for s in [k] + passes(k)[0]:
+                for c in children[s][k]:
+                    gather_copy(s, c, count).wait_send()
+                    count += 1
+    for i in range(2):
+        across[i].wait_send()
+    left(0, HALF - 1)
+    left(1, HALF)
 
 
 def body(gradient, perturbations, band_index, band_weight, wave_index, spectrum):
@@ -307,17 +348,18 @@
             pltpu.VMEM((2, 24, NDEG), F32),
             pltpu.VMEM((MEMS, GROWS, 128), BF16),
             pltpu.VMEM((48, NLON), BF16),
-            pltpu.VMEM((48, MT), BF16),
-            pltpu.VMEM((48, MT), BF16),
+            pltpu.VMEM((2, 48, 384), BF16),
+            pltpu.VMEM((2, 48, 384), BF16),
             pltpu.VMEM((2, HALF, 16, 128), BF16),
             pltpu.VMEM((2, HALF, 16, 128), BF16),
-            dma((9,)),
+            dma((10,)),
             dma((24,)),
             dma((MEMS,)),
-            dma,
-            dma,
             dma((2,)),
             dma((2,)),
+            dma((2,)),
+            dma((2,)),
+            pltpu.SemaphoreType.REGULAR,
         ],
         compiler_params=pltpu.CompilerParams(
             collective_id=0, has_side_effects=True, vmem_limit_bytes=60 * 2**20

time: 51.4 us -> 49.1 us (0.955)
  the two profiles are of different devices: /device:TPU:1 before, /device:TPU:39 now
where the time goes in v3:
time: 49.1 us; the launch traced here: 48.9 us
  Pallas kernels  47.2 us (96%)
  local copies, waits for them, and re-layouts  1.69 us (3%)
    pallas_call x1, Pallas kernels, body(): pl.pallas_call(functools.partial(kernel, trees), name='alpha_adjoint', ou...  47.2 us
    unnamed x1, local copies, waits for them, and re-layouts  1.69 us

profile of v3, /device:TPU:39, one launch (start us, length us, event | category | flops | bytes accessed | tf_op | source)
XLA Modules:
  0.0 48.9 jit_solution(6347733706689496997)
XLA Ops:
  0.0 47.2 %alpha_adjoint.1 = f32[2,2,24,768]{3,2,1,0:T(8,128)} custom-call(f32[16]{0:T(128)} %weight_s.1, bf16[6,12,2,192]{3,2,1,0:T(2,128)(2,1)} %bitcast.3, bf16[2,6,12,2,1536]{4,3,2,1,0:T(2,128)(2,1)} %bitcast.2, s32[12,1536]{1,0:T(8,128)} %band_h.1, s32[12,768]{1,0:T(8,128)} %wave_h.1, f32[2,768]{1,0:T(2,128)} %spec_h.1, ...), custom_call_target="tpu_custom_call" | custom-call | tf_op jit(solution)/shard_map/alpha_adjoint/pallas_call | solution.py:331
  47.2 1.7 %copy.12 = f32[2,2,24,768]{3,2,1,0:T(8,128)} copy(f32[2,2,24,768]{3,2,1,0:T(8,128)} %alpha_adjoint.1) | data formatting | bytes 589824

commit v4 on v3

--- a/solution.py
+++ b/solution.py
@@ -28,17 +28,19 @@
 RING = 16
 
 PARENTS = (
-    (0, 0, 1, 4, 0, 3, 4, 4),
-    (1, 1, 1, 1, 5, 2, 5, 5),
-    (2, 0, 2, 2, 6, 6, 2, 6),
-    (2, 0, 3, 3, 3, 7, 7, 3),
+    (0, 0, 0, 0, 0, 4, 4, 4),
+    (1, 1, 1, 1, 5, 1, 5, 5),
+    (2, 2, 2, 2, 6, 6, 2, 6),
+    (3, 3, 3, 3, 7, 7, 7, 3),
+    (4, 0, 0, 0, 4, 4, 4, 4),
+    (1, 5, 1, 1, 5, 5, 5, 5),
+    (2, 2, 6, 2, 6, 6, 6, 6),
+    (3, 3, 3, 7, 7, 7, 7, 7),
 )
 
 
 def gather_trees():
-    parents = [list(p) for p in PARENTS]
-    for s in reversed(range(4)):
-        parents.append([7 - PARENTS[s][7 - n] for n in range(MEMS)])
+    parents = PARENTS
     children = [
         [[c for c in range(MEMS) if c != s and parents[s][c] == n] for n in range(MEMS)] for s in range(MEMS)
     ]
@@ -55,7 +57,7 @@
         depths.append(row)
     for s in range(MEMS):
         for n in range(MEMS):
-            children[s][n].sort(key=lambda c: (-len(children[s][c]), -abs(c - n)))
+            children[s][n].sort(key=lambda c: (-len(children[s][c]), c))
     return children, depths
 
 
@@ -231,20 +233,23 @@
             alpha[:, lanes] = jnp.concatenate(rows, axis=0).astype(BF16)
 
     pl.semaphore_wait(ready, 4)
-    loads[5].wait()
-    across = []
-    for i, d in enumerate((7, -7)):
-        part = jnp.dot(alpha[...], table_v[0, :, i * 384 : i * 384 + 384], preferred_element_type=F32)
-        zsend[i] = part.astype(BF16)
-        across.append(
-            pltpu.make_async_remote_copy(
-                zsend.at[i], zrecv.at[i], as_sem.at[i], ar_sem.at[i],
-                device_id=along(d), device_id_type=MESH,
+    across = [
+        pltpu.make_async_remote_copy(
+            zsend.at[i], zrecv.at[i], as_sem.at[i], ar_sem.at[i],
+            device_id=along(d), device_id_type=MESH,
+        )
+        for i, d in enumerate((7, -7))
+    ]
+    for i in range(5, 10):
+        loads[i].wait()
+
+    def cross_over():
+        for i in range(2):
+            part = jnp.dot(
+                alpha[...], table_v[0, :, i * 384 : i * 384 + 384], preferred_element_type=F32
             )
-        )
-        across[i].start()
-    loads[6].wait()
-    mine = jnp.dot(alpha[...], table_v[1], preferred_element_type=F32).astype(BF16)
+            zsend[i] = part.astype(BF16)
+            across[i].start()
 
     lane = lax.broadcasted_iota(jnp.int32, (16, 128), 1)
 
@@ -280,21 +285,25 @@
     def left(kind, count):
         pltpu.make_async_copy(send.at[kind, 0:count], recv.at[kind, 0:count], bs_sem.at[kind]).wait()
 
-    loads[7].wait()
-    spread(mine[:, 0:384], 0, 0)
-    spread(mine[:, 384:768], 0, 16)
-    recv[0, s32] = send[0, s32]
+    def keep():
+        mine = jnp.dot(alpha[...], table_v[1], preferred_element_type=F32).astype(BF16)
+        spread(mine[:, 0:384], 0, 0)
+        spread(mine[:, 384:768], 0, 16)
+        recv[0, s32] = send[0, s32]
+
+    early = zh == 1
+    pl.when(early)(cross_over)
+    keep()
+    pl.when(jnp.logical_not(early))(cross_over)
     for i in range(2):
         across[i].wait_recv()
         spread(zrecv[i], 1, 16 * i)
 
-    loads[8].wait()
     arrived(0, HALF - 1)
     dims = (((0,), (0,)), ((), ()))
     total = lax.dot_general(
         recv[0].reshape(HALF * 16, 128), basis_v[0], dims, preferred_element_type=F32
     )
-    loads[9].wait()
     arrived(1, HALF)
     total = total + lax.dot_general(
         recv[1].reshape(HALF * 16, 128), basis_v[1], dims, preferred_element_type=F32
@@ -331,7 +340,7 @@
     return pl.pallas_call(
         functools.partial(kernel, trees),
         name="alpha_adjoint",
-        out_shape=jax.ShapeDtypeStruct((2, 2, 24, NDEG), F32),
+        out_shape=pltpu.VMEM((2, 2, 24, NDEG), F32),
         in_specs=[pl.BlockSpec(memory_space=pltpu.SMEM)] + [hbm] * 8 + [pl.BlockSpec(memory_space=pltpu.VMEM)],
         out_specs=pl.BlockSpec(memory_space=pltpu.VMEM),
         scratch_shapes=[

time: 49.1 us -> 46.8 us (0.953)
  the two profiles are of different devices: /device:TPU:39 before, /device:TPU:1 now
where the time goes in v4:
time: 46.8 us; the launch traced here: 46.6 us
  Pallas kernels  45.8 us (98%)
  local copies, waits for them, and re-layouts  0.72 us (2%)
    pallas_call x1, Pallas kernels, body(): pl.pallas_call(functools.partial(kernel, trees), name='alpha_adjoint', ou...  45.8 us

profile of v4, /device:TPU:1, one launch (start us, length us, event | category | flops | bytes accessed | tf_op | source)
XLA Modules:
  0.0 46.6 jit_solution(6822475294348896200)
XLA Ops:
  0.0 45.8 %alpha_adjoint.1 = f32[2,2,24,768]{3,2,1,0:T(8,128)S(1)} custom-call(f32[16]{0:T(128)} %weight_s.1, bf16[6,12,2,192]{3,2,1,0:T(2,128)(2,1)} %bitcast.3, bf16[2,6,12,2,1536]{4,3,2,1,0:T(2,128)(2,1)} %bitcast.2, s32[12,1536]{1,0:T(8,128)} %band_h.1, s32[12,768]{1,0:T(8,128)} %wave_h.1, f32[2,768]{1,0:T(2,128)} %spec_h.1, ...), custom_call_target="tpu_custom_call" | custom-call | tf_op jit(solution)/shard_map/alpha_adjoint/pallas_call | solution.py:340
  45.8 0.7 %copy.12 = f32[2,2,24,768]{3,2,1,0:T(8,128)} copy(f32[2,2,24,768]{3,2,1,0:T(8,128)S(1)} %alpha_adjoint.1) | data formatting | bytes 589824

commit v5 on v4

--- a/solution.py
+++ b/solution.py
@@ -95,9 +95,9 @@
 
 def kernel(
     trees,
-    weight_s, grad_h, pert_h, band_h, wave_h, spec_h, table_h, basis_h, place_h, order_v,
+    weight_h, grad_h, pert_h, band_h, wave_h, spec_h, table_h, basis_h, place_h, order_h,
     out_ref,
-    grad_v, pert_v, band_v, wave_v, spec_v, table_v, basis_v, place_v,
+    weight_s, grad_v, pert_v, band_v, wave_v, spec_v, table_v, basis_v, place_v, order_v,
     gpack, area, factor, gbuf, alpha, zsend, zrecv, send, recv,
     load_sem, gs_sem, gr_sem, as_sem, ar_sem, bs_sem, br_sem, ready,
 ):
@@ -115,11 +115,10 @@
         (grad_h.reshape(ROWS, 192), grad_v), (band_h, band_v), (wave_h, wave_v), (spec_h, spec_v),
         (pert_h.reshape(2, ROWS, NLON), pert_v), (table_h.at[1 - zh], table_v.at[0]),
         (table_h.at[zh], table_v.at[1]), (place_h, place_v), (basis_h.at[zh], basis_v.at[0]),
-        (basis_h.at[1 - zh], basis_v.at[1]),
+        (basis_h.at[1 - zh], basis_v.at[1]), (order_h, order_v), (weight_h, weight_s),
     ]
     loads = [pltpu.make_async_copy(a, b, load_sem.at[i]) for i, (a, b) in enumerate(loads)]
-    for c in loads:
-        c.start()
+    loads[0].start()
 
     barrier = pltpu.get_barrier_semaphore()
     for d in (4, -4, 3, -3, 2, -2, 1, -1):
@@ -132,6 +131,8 @@
         return 0
 
     lax.fori_loop(1, HALF, greet_half, 0)
+    for c in [loads[11]] + loads[1:11]:
+        c.start()
 
     loads[0].wait()
     gpack[:, 0:192] = grad_v[...].astype(F32)
@@ -171,6 +172,7 @@
         pl.semaphore_signal(ready, inc=1, device_id=along(d), device_id_type=MESH)
 
     loads[1].wait()
+    loads[11].wait()
     band = band_v[...]
     a = jnp.zeros((CYC, NLON), F32)
     for b in range(16):
@@ -240,7 +242,7 @@
         )
         for i, d in enumerate((7, -7))
     ]
-    for i in range(5, 10):
+    for i in range(5, 11):
         loads[i].wait()
 
     def cross_over():
@@ -341,9 +343,10 @@
         functools.partial(kernel, trees),
         name="alpha_adjoint",
         out_shape=pltpu.VMEM((2, 2, 24, NDEG), F32),
-        in_specs=[pl.BlockSpec(memory_space=pltpu.SMEM)] + [hbm] * 8 + [pl.BlockSpec(memory_space=pltpu.VMEM)],
+        in_specs=[hbm] * 10,
         out_specs=pl.BlockSpec(memory_space=pltpu.VMEM),
         scratch_shapes=[
+            pltpu.SMEM(band_weight.shape, F32),
             pltpu.VMEM((ROWS, 192), BF16),
             pltpu.VMEM((2, ROWS, NLON), BF16),
             pltpu.VMEM(band_index.shape, jnp.int32),
@@ -352,6 +355,7 @@
             pltpu.VMEM(table.shape, BF16),
             pltpu.VMEM(basis.shape, BF16),
             pltpu.VMEM(place.shape, BF16),
+            pltpu.VMEM(order.shape, BF16),
             pltpu.VMEM((ROWS, 256), F32),
             pltpu.VMEM((24, NLON), F32),
             pltpu.VMEM((2, 24, NDEG), F32),
@@ -361,7 +365,7 @@
             pltpu.VMEM((2, 48, 384), BF16),
             pltpu.VMEM((2, HALF, 16, 128), BF16),
             pltpu.VMEM((2, HALF, 16, 128), BF16),
-            dma((10,)),
+            dma((12,)),
             dma((24,)),
             dma((MEMS,)),
             dma((2,)),

time: 46.8 us -> 46.1 us (0.985)
  Pallas kernels: 45.8 us -> 45.1 us
    pallas_call x1, Pallas kernels: 45.8 us -> 45.1 us  [body(): pl.pallas_call(functools.partial(kernel, trees), name='alpha_adjoint', ou...]
where the time goes in v5:
time: 46.1 us; the launch traced here: 45.9 us
  Pallas kernels  45.1 us (98%)
  local copies, waits for them, and re-layouts  0.72 us (2%)
    pallas_call x1, Pallas kernels, body(): pl.pallas_call(functools.partial(kernel, trees), name='alpha_adjoint', ou...  45.1 us

profile of v5, /device:TPU:1, one launch (start us, length us, event | category | flops | bytes accessed | tf_op | source)
XLA Modules:
  0.0 45.9 jit_solution(17180879143844173527)
XLA Ops:
  0.0 45.1 %alpha_adjoint.1 = f32[2,2,24,768]{3,2,1,0:T(8,128)S(1)} custom-call(f32[16]{0:T(128)} %weight_h.1, bf16[6,12,2,192]{3,2,1,0:T(2,128)(2,1)} %bitcast.3, bf16[2,6,12,2,1536]{4,3,2,1,0:T(2,128)(2,1)} %bitcast.2, s32[12,1536]{1,0:T(8,128)} %band_h.1, s32[12,768]{1,0:T(8,128)} %wave_h.1, f32[2,768]{1,0:T(2,128)} %spec_h.1, ...), custom_call_target="tpu_custom_call" | custom-call | tf_op jit(solution)/shard_map/alpha_adjoint/pallas_call | solution.py:342
  45.1 0.7 %copy.12 = f32[2,2,24,768]{3,2,1,0:T(8,128)} copy(f32[2,2,24,768]{3,2,1,0:T(8,128)S(1)} %alpha_adjoint.1) | data formatting | bytes 589824

commit v6 on v5

--- a/solution.py
+++ b/solution.py
@@ -28,14 +28,14 @@
 RING = 16
 
 PARENTS = (
-    (0, 0, 0, 0, 0, 4, 4, 4),
-    (1, 1, 1, 1, 5, 1, 5, 5),
-    (2, 2, 2, 2, 6, 6, 2, 6),
-    (3, 3, 3, 3, 7, 7, 7, 3),
-    (4, 0, 0, 0, 4, 4, 4, 4),
-    (1, 5, 1, 1, 5, 5, 5, 5),
-    (2, 2, 6, 2, 6, 6, 6, 6),
-    (3, 3, 3, 7, 7, 7, 7, 7),
+    (0, 0, 0, 2, 0, 4, 4, 6),
+    (1, 1, 1, 2, 5, 1, 5, 6),
+    (1, 2, 2, 2, 5, 6, 2, 6),
+    (1, 3, 3, 3, 5, 7, 7, 3),
+    (4, 0, 0, 2, 4, 4, 4, 6),
+    (1, 5, 1, 2, 5, 5, 5, 6),
+    (1, 2, 6, 2, 5, 6, 6, 6),
+    (1, 3, 3, 7, 5, 7, 7, 7),
 )
 
 
@@ -168,8 +168,7 @@
             for i, c in enumerate(children[k][k]):
                 gather_copy(k, c, i).start()
 
-    for d in (4, -4, 1, -1):
-        pl.semaphore_signal(ready, inc=1, device_id=along(d), device_id_type=MESH)
+    pl.semaphore_signal(ready, inc=1, device_id=along(-4), device_id_type=MESH)
 
     loads[1].wait()
     loads[11].wait()
@@ -234,13 +233,13 @@
                 rows.append(area[:, lanes] * acc)
             alpha[:, lanes] = jnp.concatenate(rows, axis=0).astype(BF16)
 
-    pl.semaphore_wait(ready, 4)
+    pl.semaphore_wait(ready, 1)
     across = [
         pltpu.make_async_remote_copy(
             zsend.at[i], zrecv.at[i], as_sem.at[i], ar_sem.at[i],
-            device_id=along(d), device_id_type=MESH,
-        )
-        for i, d in enumerate((7, -7))
+            device_id=along(8), device_id_type=MESH,
+        )
+        for i in range(2)
     ]
     for i in range(5, 11):
         loads[i].wait()
@@ -255,10 +254,10 @@
 
     lane = lax.broadcasted_iota(jnp.int32, (16, 128), 1)
 
-    def message(kind, slot, to):
+    def message(kind, slot):
         return pltpu.make_async_remote_copy(
             send.at[kind, slot], recv.at[kind, s32], bs_sem.at[kind], br_sem.at[kind],
-            device_id=to, device_id_type=MESH,
+            device_id=(m, zh * HALF + slot), device_id_type=MESH,
         )
 
     def spread(part, kind, base):
@@ -274,18 +273,14 @@
                     whole = moved if whole is None else jnp.where(lane >= 32 * el, moved, whole)
                 slot = base + 4 * t + d
                 send[kind, slot] = whole.astype(BF16)
-                if kind == 0:
-                    @pl.when(s32 != slot)
-                    def _(slot=slot):
-                        message(0, slot, (m, zh * HALF + slot)).start()
-                else:
-                    message(1, slot, along(1 if base == 0 else -1, slot)).start()
-
-    def arrived(kind, count):
-        pltpu.make_async_copy(send.at[kind, 0:count], recv.at[kind, 0:count], br_sem.at[kind]).wait()
-
-    def left(kind, count):
-        pltpu.make_async_copy(send.at[kind, 0:count], recv.at[kind, 0:count], bs_sem.at[kind]).wait()
+
+                @pl.when(s32 != slot)
+                def _(slot=slot):
+                    message(kind, slot).start()
+
+    def arrived(kind, sem):
+        count = HALF - 1
+        pltpu.make_async_copy(send.at[kind, 0:count], recv.at[kind, 0:count], sem.at[kind]).wait()
 
     def keep():
         mine = jnp.dot(alpha[...], table_v[1], preferred_element_type=F32).astype(BF16)
@@ -301,12 +296,13 @@
         across[i].wait_recv()
         spread(zrecv[i], 1, 16 * i)
 
-    arrived(0, HALF - 1)
+    recv[1, s32] = send[1, s32]
+    arrived(0, br_sem)
     dims = (((0,), (0,)), ((), ()))
     total = lax.dot_general(
         recv[0].reshape(HALF * 16, 128), basis_v[0], dims, preferred_element_type=F32
     )
-    arrived(1, HALF)
+    arrived(1, br_sem)
     total = total + lax.dot_general(
         recv[1].reshape(HALF * 16, 128), basis_v[1], dims, preferred_element_type=F32
     )
@@ -325,8 +321,8 @@
                     count += 1
     for i in range(2):
         across[i].wait_send()
-    left(0, HALF - 1)
-    left(1, HALF)
+    arrived(0, bs_sem)
+    arrived(1, bs_sem)
 
 
 def body(gradient, perturbations, band_index, band_weight, wave_index, spectrum):

time: 46.1 us -> 45.7 us (level)
  no operation moved by 1% of the time
where the time goes in v6:
time: 45.7 us; the launch traced here: 45.5 us
  Pallas kernels  44.8 us (98%)
  local copies, waits for them, and re-layouts  0.72 us (2%)
    pallas_call x1, Pallas kernels, body(): pl.pallas_call(functools.partial(kernel, trees), name='alpha_adjoint', ou...  44.8 us

profile of v6, /device:TPU:1, one launch (start us, length us, event | category | flops | bytes accessed | tf_op | source)
XLA Modules:
  0.0 45.5 jit_solution(1651265763720189117)
XLA Ops:
  0.0 44.8 %alpha_adjoint.1 = f32[2,2,24,768]{3,2,1,0:T(8,128)S(1)} custom-call(f32[16]{0:T(128)} %weight_h.1, bf16[6,12,2,192]{3,2,1,0:T(2,128)(2,1)} %bitcast.3, bf16[2,6,12,2,1536]{4,3,2,1,0:T(2,128)(2,1)} %bitcast.2, s32[12,1536]{1,0:T(8,128)} %band_h.1, s32[12,768]{1,0:T(8,128)} %wave_h.1, f32[2,768]{1,0:T(2,128)} %spec_h.1, ...), custom_call_target="tpu_custom_call" | custom-call | tf_op jit(solution)/shard_map/alpha_adjoint/pallas_call | solution.py:338
  44.8 0.7 %copy.12 = f32[2,2,24,768]{3,2,1,0:T(8,128)} copy(f32[2,2,24,768]{3,2,1,0:T(8,128)S(1)} %alpha_adjoint.1) | data formatting | bytes 589824

commit v7 on v6

--- a/solution.py
+++ b/solution.py
@@ -28,14 +28,14 @@
 RING = 16
 
 PARENTS = (
-    (0, 0, 0, 2, 0, 4, 4, 6),
-    (1, 1, 1, 2, 5, 1, 5, 6),
-    (1, 2, 2, 2, 5, 6, 2, 6),
-    (1, 3, 3, 3, 5, 7, 7, 3),
-    (4, 0, 0, 2, 4, 4, 4, 6),
-    (1, 5, 1, 2, 5, 5, 5, 6),
-    (1, 2, 6, 2, 5, 6, 6, 6),
-    (1, 3, 3, 7, 5, 7, 7, 7),
+    (0, 0, 0, 2, 0, 4, 4, 4),
+    (1, 1, 1, 2, 5, 1, 5, 5),
+    (1, 2, 2, 2, 6, 6, 2, 6),
+    (1, 3, 3, 3, 7, 7, 7, 3),
+    (4, 0, 0, 0, 4, 4, 4, 6),
+    (1, 5, 1, 1, 5, 5, 5, 6),
+    (2, 2, 6, 2, 5, 6, 6, 6),
+    (3, 3, 3, 7, 5, 7, 7, 7),
 )
 
 

time: 45.7 us -> 45 us (0.985); the launches traced: 45.5 us -> 44.3 us
  Pallas kernels: 44.8 us -> 43.6 us
    pallas_call x1, Pallas kernels: 44.8 us -> 43.6 us  [body(): pl.pallas_call(functools.partial(kernel, trees), name='alpha_adjoint', ou...]
where the time goes in v7:
time: 45 us; the launch traced here: 44.3 us
  Pallas kernels  43.6 us (97%)
  local copies, waits for them, and re-layouts  0.72 us (2%)
    pallas_call x1, Pallas kernels, body(): pl.pallas_call(functools.partial(kernel, trees), name='alpha_adjoint', ou...  43.6 us

profile of v7, /device:TPU:1, one launch (start us, length us, event | category | flops | bytes accessed | tf_op | source)
XLA Modules:
  0.0 44.3 jit_solution(11672165880674704816)
XLA Ops:
  0.0 43.6 %alpha_adjoint.1 = f32[2,2,24,768]{3,2,1,0:T(8,128)S(1)} custom-call(f32[16]{0:T(128)} %weight_h.1, bf16[6,12,2,192]{3,2,1,0:T(2,128)(2,1)} %bitcast.3, bf16[2,6,12,2,1536]{4,3,2,1,0:T(2,128)(2,1)} %bitcast.2, s32[12,1536]{1,0:T(8,128)} %band_h.1, s32[12,768]{1,0:T(8,128)} %wave_h.1, f32[2,768]{1,0:T(2,128)} %spec_h.1, ...), custom_call_target="tpu_custom_call" | custom-call | tf_op jit(solution)/shard_map/alpha_adjoint/pallas_call | solution.py:338
  43.6 0.7 %copy.12 = f32[2,2,24,768]{3,2,1,0:T(8,128)} copy(f32[2,2,24,768]{3,2,1,0:T(8,128)S(1)} %alpha_adjoint.1) | data formatting | bytes 589824

commit v8 on v7

--- a/solution.py
+++ b/solution.py
@@ -131,9 +131,6 @@
         return 0
 
     lax.fori_loop(1, HALF, greet_half, 0)
-    for c in [loads[11]] + loads[1:11]:
-        c.start()
-
     loads[0].wait()
     gpack[:, 0:192] = grad_v[...].astype(F32)
     lane = lax.broadcasted_iota(jnp.int32, (ROWS, 128), 1)
@@ -169,6 +166,9 @@
                 gather_copy(k, c, i).start()
 
     pl.semaphore_signal(ready, inc=1, device_id=along(-4), device_id_type=MESH)
+
+    for c in [loads[11]] + loads[1:11]:
+        c.start()
 
     loads[1].wait()
     loads[11].wait()

time: 45 us -> 45 us (level)
  no operation moved by 1% of the time
where the time goes in v8:
time: 45 us; the launch traced here: 44.3 us
  Pallas kernels  43.6 us (97%)
  local copies, waits for them, and re-layouts  0.72 us (2%)
    pallas_call x1, Pallas kernels, body(): pl.pallas_call(functools.partial(kernel, trees), name='alpha_adjoint', ou...  43.6 us

profile of v8, /device:TPU:1, one launch (start us, length us, event | category | flops | bytes accessed | tf_op | source)
XLA Modules:
  0.0 44.3 jit_solution(14427766650875309240)
XLA Ops:
  0.0 43.6 %alpha_adjoint.1 = f32[2,2,24,768]{3,2,1,0:T(8,128)S(1)} custom-call(f32[16]{0:T(128)} %weight_h.1, bf16[6,12,2,192]{3,2,1,0:T(2,128)(2,1)} %bitcast.3, bf16[2,6,12,2,1536]{4,3,2,1,0:T(2,128)(2,1)} %bitcast.2, s32[12,1536]{1,0:T(8,128)} %band_h.1, s32[12,768]{1,0:T(8,128)} %wave_h.1, f32[2,768]{1,0:T(2,128)} %spec_h.1, ...), custom_call_target="tpu_custom_call" | custom-call | tf_op jit(solution)/shard_map/alpha_adjoint/pallas_call | solution.py:338
  43.6 0.7 %copy.12 = f32[2,2,24,768]{3,2,1,0:T(8,128)} copy(f32[2,2,24,768]{3,2,1,0:T(8,128)S(1)} %alpha_adjoint.1) | data formatting | bytes 589824
